TPU v7x, 256 devices: a whole 4x4x8 slice. The times are simulated.
256 devices in a mesh: layer: 8 (over z_lo, y), feat: 32 (over z_hi, x, core).
Axes of the slice: x: 4, y: 4, z: 8 (z_hi: 4, z_lo: 2; z = z_hi * 2 + z_lo), core: 2. Of those that a mesh axis runs over, the one named last changes fastest.
Arguments:
- source: bfloat16 [512, 4096], P(None, 'layer'), may hold values from -6 to 6
- enc_weight: bfloat16 [4096, 16384], P('layer', 'feat'), may hold values from -0.09375 to 0.09375
- enc_bias: float32 [16384], P('feat'), may hold values from -0.5 to 0.5
- dec_weight: bfloat16 [8, 16384, 4096], P('layer', 'feat'), may hold values from -0.046875 to 0.046875
- dec_bias: float32 [8, 4096], P('layer'), may hold values from -3 to 3
- target: bfloat16 [8, 512, 4096], P('layer'), may hold values from -36 to 36
Outputs:
- grad_enc: float32 [4096, 16384], P('layer', 'feat')
- grad_enc_bias: float32 [16384], P('feat')
- grad_dec: bfloat16 [8, 16384, 4096], P('layer', 'feat')
- grad_dec_bias: float32 [8, 4096], P('layer', 'feat')
- loss: float32 [], replicated
All inputs are finite; a program needn't handle non-finite values.
Results may differ from a plain program's by a relative error of at most 0.0049.
Values may be sent and summed in bfloat16 or wider, within the bound.
A program may use at most 128 MiB of HBM per device.

v0:
```python
import jax
import jax.numpy as jnp
from jax import lax
from jax.sharding import PartitionSpec as P


def activate(pre):
    return jax.nn.gelu(pre, approximate=True)


def shards(source, enc_weight, enc_bias, dec_weight, dec_bias, target):
    partial_pre = jnp.dot(source, enc_weight, preferred_element_type=jnp.float32)
    pre = lax.psum(partial_pre, "layer") + enc_bias
    acts = activate(pre).astype(jnp.bfloat16)
    weight = dec_weight[0]
    width = weight.shape[1]
    tok_rows = source.shape[0]
    columns = width // lax.axis_size("feat")
    first = lax.axis_index("feat") * columns
    partial_rec = jnp.dot(acts, weight, preferred_element_type=jnp.float32)
    recon = lax.psum(partial_rec, "feat") + dec_bias[0]
    err = recon - target[0].astype(jnp.float32)
    err_own = lax.dynamic_slice_in_dim(err, first, columns, 1)
    err_b = err.astype(jnp.bfloat16)
    grad_w = lax.dot_general(
        acts, err_b, (((0,), (0,)), ((), ())), preferred_element_type=jnp.float32
    )
    back = lax.dot_general(
        err_b, weight, (((1,), (1,)), ((), ())), preferred_element_type=jnp.float32
    )
    grad_dec = grad_w.astype(jnp.bfloat16)[None]
    grad_dec_bias = jnp.sum(err_own, axis=0)[None]
    squares = lax.psum(jnp.sum(err_own * err_own), ("layer", "feat"))
    layers = lax.axis_size("layer") * dec_weight.shape[0]
    loss = squares / (2.0 * tok_rows * layers * width)
    back_total = lax.psum(back, "layer")
    _, pullback = jax.vjp(activate, pre)
    dpre = pullback(back_total)[0]
    grad_enc_bias = jnp.sum(dpre, axis=0)
    grad_enc = lax.dot_general(
        source,
        dpre.astype(jnp.bfloat16),
        (((0,), (0,)), ((), ())),
        preferred_element_type=jnp.float32,
    )
    return (grad_enc, grad_enc_bias, grad_dec, grad_dec_bias, loss)


def solution(mesh):
    return jax.shard_map(
        shards,
        mesh=mesh,
        in_specs=(
            P(None, "layer"),
            P("layer", "feat"),
            P("feat"),
            P("layer", "feat", None),
            P("layer", None),
            P("layer", None, None),
        ),
        out_specs=(
            P("layer", "feat"),
            P("feat"),
            P("layer", "feat", None),
            P("layer", "feat"),
            P(),
        ),
        check_vma=False,
    )
```

profile of v0, /device:TPU:1, one launch (start us, length us, event | category | flops | bytes accessed | tf_op | source)
XLA Modules:
  0.0 550.6 jit_solution(14404257698108874329)
XLA Ops:
  7.2 0.0 copy-start
  7.2 0.0 all-reduce.4.cloned.1.call-start
  7.2 1.0 copy-done
  8.2 2.4 fusion.16
  10.7 0.0 all-reduce.4.cloned.1.call-update
  10.7 0.0 copy-start.4
  10.7 0.0 all-reduce.6.cloned.1.call-start
  10.7 81.6 %all-reduce.4.cloned.1.call-done = f32[512,512]{1,0:T(8,128)} async-done(((f32[512,512]{1,0:T(8,128)}), f32[512,512]{1,0:T(8,128)}) %all-reduce.4.cloned.1.call-update) | async-done | bytes 1048592 | tf_op jit(solution)/shard_map/psum | solution.py:13
  92.3 8.2 %fusion.3 = f32[512,4096]{1,0:T(8,128)} fusion(bf16[1,512,4096]{2,1,0:T(8,128)(2,1)} %param.9, f32[512,512]{1,0:T(8,128)} %all-reduce.4.cloned.1.call-done, f32[512]{0:T(512)} %param.8), kind=kOutput, calls=%fused_computation.5 | convolution fusion | flops 2150105088 | bytes 13633536 | tf_op jit(solution)/shard_map/dot_general | solution.py:20
  100.6 0.0 all-reduce.6.cloned.1.call-update
  100.6 0.0 all-reduce.8.cloned.1.call-start
  100.7 329.5 %all-reduce.6.cloned.1.call-done = f32[512,4096]{1,0:T(8,128)} async-done(((f32[512,4096]{1,0:T(8,128)}), f32[512,4096]{1,0:T(8,128)}) %all-reduce.6.cloned.1.call-update) | async-done | bytes 8388624 | tf_op jit(solution)/shard_map/psum | solution.py:21
  430.2 0.0 copy-done.4
  430.2 5.8 %convert_subtract_fusion = f32[512,4096]{1,0:T(8,128)S(1)} fusion(f32[512,4096]{1,0:T(8,128)} %all-reduce.6.cloned.1.call-done, bf16[1,512,4096]{2,1,0:T(8,128)(2,1)} %param.11, f32[4096]{0:T(1024)S(1)} %bitcast.18), kind=kLoop, calls=%fused_computation | loop fusion | flops 6291456 | bytes 20987904 | tf_op jit(solution)/shard_map/sub | solution.py:22
  436.0 0.0 copy-start.1
  436.0 3.2 copy-done.1
  439.2 0.0 copy-start.2
  439.2 0.0 copy-start.3
  439.2 5.6 %fusion.1 = f32[512,512]{1,0:T(8,128)} fusion(bf16[1,512,4096]{2,1,0:T(8,128)(2,1)} %param.9, f32[512,4096]{1,0:T(8,128)S(1)} %convert_subtract_fusion), kind=kOutput, calls=%fused_computation.3 | convolution fusion | flops 2149580800 | bytes 13631488 | tf_op jit(solution)/shard_map/dot_general | solution.py:28
  444.8 0.0 all-reduce.8.cloned.1.call-update
  444.8 1.6 multiply_reduce_fusion
  446.5 83.6 %psum.31 = f32[]{:T(128)} all-reduce(f32[]{:T(128)} %get-tuple-element.10), channel_id=1, replica_groups=mesh['layer'=8,'feat'=32] {'layer','feat'}, use_global_device_ids=true, to_apply=%region_6.0 | all-reduce | flops 1 | bytes 8 | tf_op jit(solution)/shard_map/psum | solution.py:33
  530.7 0.0 copy-done.2
  530.7 0.0 copy-done.3
  530.7 7.9 %fusion = bf16[1,512,4096]{2,1,0:T(8,128)(2,1)} fusion(f32[512,4096]{1,0:T(8,128)} %copy-done.1, f32[512,512]{1,0:T(8,128)S(1)} %copy-done.2, f32[512]{0:T(512)S(1)} %copy-done.3), kind=kOutput, calls=%fused_computation.2 | convolution fusion | flops 2154299392 | bytes 13633536 | tf_op jit(solution)/shard_map/dot_general | solution.py:25
  538.6 0.0 all-reduce.8.cloned.1.call-done
  538.6 2.6 fusion.14
  541.2 0.5 convolution_bitcast_fusion
  541.6 1.3 copy.11
Async XLA Ops:
  7.2 1.0 copy-start
  7.2 85.2 %all-reduce.4.cloned.1.call-start = ((), (), s32[]{:S(2)}) async-start(), calls=%async_computation | async-start | bytes 2097152 | tf_op jit(solution)/shard_map/psum | solution.py:13
  10.7 419.5 %copy-start.4 = (f32[1,4096]{1,0:T(1,128)S(1)}, f32[1,4096]{1,0:T(1,128)}, u32[]{:S(2)}) copy-start(f32[1,4096]{1,0:T(1,128)} %param.10) | copy-start | bytes 49156
  10.7 419.5 %all-reduce.6.cloned.1.call-start = ((), (), s32[]{:S(2)}) async-start(), calls=%async_computation.1 | async-start | bytes 16777216 | tf_op jit(solution)/shard_map/psum | solution.py:21
  100.6 438.0 %all-reduce.8.cloned.1.call-start = ((), (), s32[]{:S(2)}) async-start(), calls=%async_computation.2 | async-start | bytes 2097152 | tf_op jit(solution)/shard_map/psum | solution.py:36
  436.0 3.2 copy-start.1
  439.2 91.5 %copy-start.2 = (f32[512,512]{1,0:T(8,128)S(1)}, f32[512,512]{1,0:T(8,128)}, u32[]{:S(2)}) copy-start(f32[512,512]{1,0:T(8,128)} %all-reduce.4.cloned.1.call-done) | copy-start | bytes 3145732
  439.2 91.5 %copy-start.3 = (f32[512]{0:T(512)S(1)}, f32[512]{0:T(512)}, u32[]{:S(2)}) copy-start(f32[512]{0:T(512)} %param.8) | copy-start | bytes 6148
Sparse Core Ops, SparseCore 0:
  11.2 81.0 all-reduce.3
  100.7 329.4 all-reduce.5
  445.0 79.1 all-reduce.7
where the time goes:
time: 551 us
  waiting for transfers between devices  411 us (75%)
  blocking collectives  83.6 us (15%)
  matrix products  24.6 us (4%)
  between operations  15.6 us (3%)
  other arithmetic  9.98 us (2%)
  local copies, waits for them, and re-layouts  5.53 us (1%)
    psum x1, waiting for transfers between devices, shards(): recon = lax.psum(partial_rec, 'feat') + dec_bias[0]  330 us
    psum x1, blocking collectives, shards(): squares = lax.psum(jnp.sum(err_own * err_own), ('layer', 'feat'))  83.6 us
    psum x1, waiting for transfers between devices, shards(): pre = lax.psum(partial_pre, 'layer') + enc_bias  81.6 us
  transfers between devices with their start and end apart: 3, of which 2 were waited for; matrix products, arithmetic and copies ran while one was open for 2% of the time, Pallas kernels for 0%

commit v1 on v0

v1 whole, which is shorter than its diff:
```python
import functools

import jax
import jax.numpy as jnp
from jax import lax
from jax.experimental import pallas as pl
from jax.experimental.pallas import tpu as pltpu
from jax.sharding import PartitionSpec as P

BF = jnp.bfloat16
F32 = jnp.float32
MESH = pl.DeviceIdType.MESH

NY, NX, NZ = 4, 4, 4
CHUNK = 64
LAG = dict(P1=0, P2=1, P3=2, P4=3, P5=4, P6A=5, P6=6, P7=7, P8=8, P8A=9, P9=10, P10=11, P11=12, P12=13, P13=14)
ORDER = ("P13", "P12", "P11", "P10", "P9", "P8A", "P8", "P7", "P6", "P6A", "P5", "P4", "P3", "P2", "P1")
KINDS = ("YR", "ZP", "YA", "SA", "HP", "HM", "OP", "OM", "AP", "AM", "ZR", "ZA", "XP", "XM", "FP", "FM", "SB", "YB", "ZB", "YD")
ID = {name: i for i, name in enumerate(KINDS)}
ONCE = ("W", "GB", "L1", "L2", "L3", "L4", "L5", "GD")
OID = {name: i for i, name in enumerate(ONCE)}
A0 = 0.7978845608
A1 = 0.044715


def dot(a, b, dims):
    return lax.dot_general(a, b, (dims, ((), ())), preferred_element_type=F32)


def kernel(
    src_h, enc_h, encb_v, w_h, decb_v, tgt_h,
    ge_v, geb_v, gd_h, gdb_v, loss_s,
    src, enc, tgt, w, ps, ry, zs_p, zr_p, gpr, acts, rec, own, hp, hm, op, om, ap, am, sp, sm, zsend, zown, rz, eall,
    b_own, b_send, b_recv, by, ryb, zs_b, zr_b, dall, gd, pb, rpb, sq, rl1, rl2, rl3, rl4, rl5, sl2, sl3, sl4, sl5, bsum,
    lsem, ssem, rsem, oss, ors,
):
    tok, depth = src.shape
    feats = enc.shape[1]
    half = w.shape[1]
    tt = CHUNK
    nch = tok // tt
    rows = tt // NY
    group = half // NX
    hg = group // 2
    blk = group // NZ
    lay, fea = lax.axis_index("layer"), lax.axis_index("feat")
    zl, y = lay // NY, lay % NY
    zh, x, core = fea // (2 * NX), (fea // 2) % NX, fea % 2

    def dev(dzl=0, dy=0, dzh=0, dx=0, dc=0):
        return (
            ((zl + dzl) % 2) * NY + (y + dy) % NY,
            ((zh + dzh) % NZ) * (2 * NX) + ((x + dx) % NX) * 2 + (core + dc) % 2,
        )

    def send(kind, k, src_ref, dst_ref, to):
        pltpu.make_async_remote_copy(
            src_ref, dst_ref, ssem.at[ID[kind]], rsem.at[ID[kind], k], device_id=to, device_id_type=MESH
        ).start()

    def got(kind, k, ref):
        pltpu.make_async_copy(ref, ref, rsem.at[ID[kind], k]).wait()

    def send1(kind, src_ref, dst_ref, to):
        pltpu.make_async_remote_copy(
            src_ref, dst_ref, oss.at[OID[kind]], ors.at[OID[kind]], device_id=to, device_id_type=MESH
        ).start()

    def got1(kind, ref):
        pltpu.make_async_copy(ref, ref, ors.at[OID[kind]]).wait()

    barrier = pltpu.get_barrier_semaphore()
    peers = (
        [dict(dy=o) for o in range(1, NY)] + [dict(dzl=1), dict(dc=1)]
        + [dict(dx=o) for o in range(1, NX)] + [dict(dzh=o) for o in range(1, NZ)]
    )
    for p in peers:
        pl.semaphore_signal(barrier, inc=1, device_id=dev(**p), device_id_type=MESH)

    c_src = pltpu.make_async_copy(src_h, src, lsem.at[0])
    c_enc = pltpu.make_async_copy(enc_h, enc, lsem.at[1])
    c_src.start()
    c_enc.start()

    def column(o, p, c):
        return pl.multiple_of((((zh + p) % NZ) * (2 * NX) + ((x + o) % NX) * 2 + c) * blk, blk)

    for o in range(NX):
        for p in range(NZ):
            pltpu.make_async_copy(
                w_h.at[0, :, pl.ds(column(o, p, core), blk)],
                w.at[pl.ds(0, feats), pl.ds((o * NZ + p) * blk, blk)],
                lsem.at[2],
            ).start()
    c_tgt = pltpu.make_async_copy(tgt_h.at[0, :, pl.ds(pl.multiple_of(fea * blk, blk), blk)], tgt, lsem.at[3])
    c_tgt.start()
    pl.semaphore_wait(barrier, len(peers))
    for o in range(NX):
        for p in range(NZ):
            send1(
                "W", w_h.at[0, :, pl.ds(column(o, p, 1 - core), blk)],
                w.at[pl.ds(feats, feats), pl.ds((o * NZ + p) * blk, blk)], dev(dc=1),
            )
    sq[...] = jnp.zeros_like(sq)
    pb[...] = jnp.zeros_like(pb)
    bsum[...] = jnp.zeros_like(bsum)
    c_src.wait()
    c_enc.wait()

    def span(k):
        return pl.ds(pl.multiple_of(k * tt, tt), tt)

    def piece(k, yy):
        return pl.ds(pl.multiple_of(k * tt + yy * rows, rows), rows)

    def fold(v):
        return jnp.sum(v.reshape(v.shape[0] // 8, 8, v.shape[1]), axis=0)

    def p1(k):
        ps[span(k)] = dot(src[span(k)], enc[...], ((1,), (0,)))
        for o in range(1, NY):
            send("YR", k, ps.at[piece(k, (y + o) % NY)], ry.at[k, o - 1], dev(dy=o))

    def p2(k):
        got("YR", k, ry.at[k])
        zs_p[k] = ps[piece(k, y)] + ry[k, 0] + ry[k, 1] + ry[k, 2]
        send("ZP", k, zs_p.at[k], zr_p.at[k], dev(dzl=1))

    def p3(k):
        got("ZP", k, zr_p.at[k])
        v = zs_p[k] + zr_p[k] + encb_v[...]
        v2 = v * v
        t = jnp.tanh(A0 * (v * (1.0 + A1 * v2)))
        h = 0.5 * (1.0 + t)
        acts[piece(k, y), pl.ds(0, feats)] = (v * h).astype(BF)
        for o in range(1, NY):
            r = acts.at[piece(k, y), pl.ds(0, feats)]
            send("YA", k, r, r, dev(dy=o))
        gpr[k] = h + 0.5 * v * (1.0 - t * t) * (A0 * (1.0 + 3.0 * A1 * v2))

    def p4(k):
        got("YA", k, acts.at[pl.ds(0, 3 * rows), pl.ds(0, feats)])
        send("SA", k, acts.at[span(k), pl.ds(0, feats)], acts.at[span(k), pl.ds(feats, feats)], dev(dc=1))

    def p5(k):
        got("SA", k, acts.at[span(k), pl.ds(feats, feats)])

        @pl.when(k == 0)
        def _():
            pltpu.make_async_copy(w.at[pl.ds(0, feats)], w.at[pl.ds(0, feats)], lsem.at[2]).wait()
            got1("W", w.at[pl.ds(feats, feats)])

        a = acts[span(k)]
        s = span(k)
        for o in (2, 1, 3):
            rec[s, pl.ds(o * group, group)] = dot(a, w[:, pl.ds(o * group, group)], ((1,), (0,))).astype(BF)
            if o == 2:
                send("HP", k, rec.at[s, pl.ds(2 * group, hg)], hp.at[s], dev(dx=1))
                send("HM", k, rec.at[s, pl.ds(2 * group + hg, hg)], hm.at[s], dev(dx=3))
            elif o == 1:
                send("OP", k, rec.at[s, pl.ds(group + hg, hg)], op.at[s], dev(dx=1))
            else:
                send("OM", k, rec.at[s, pl.ds(3 * group, hg)], om.at[s], dev(dx=3))
        own[s] = dot(a, w[:, pl.ds(0, group)], ((1,), (0,)))

    def p6a(k):
        s = span(k)
        got("HP", k, hp.at[s])
        sp[s] = (hp[s].astype(F32) + rec[s, pl.ds(group, hg)].astype(F32)).astype(BF)
        send("AP", k, sp.at[s], ap.at[s], dev(dx=1))
        got("HM", k, hm.at[s])
        sm[s] = (hm[s].astype(F32) + rec[s, pl.ds(3 * group + hg, hg)].astype(F32)).astype(BF)
        send("AM", k, sm.at[s], am.at[s], dev(dx=3))

    def p6(k):
        s = span(k)
        got("OP", k, op.at[s])
        got("OM", k, om.at[s])
        got("AP", k, ap.at[s])
        got("AM", k, am.at[s])
        first = own[s, pl.ds(0, hg)] + ap[s].astype(F32) + om[s].astype(F32)
        second = own[s, pl.ds(hg, hg)] + am[s].astype(F32) + op[s].astype(F32)
        zown[s] = first[:, :blk]
        zsend[s, pl.ds(0, hg)] = first.astype(BF)
        zsend[s, pl.ds(hg, hg)] = second.astype(BF)
        for p in range(1, NZ):
            send("ZR", k, zsend.at[s, pl.ds(p * blk, blk)], rz.at[k, p - 1], dev(dzh=p))

    def p7(k):
        s = span(k)
        got("ZR", k, rz.at[k])
        recon = zown[s] + rz[k, 0].astype(F32) + rz[k, 1].astype(F32) + rz[k, 2].astype(F32)

        @pl.when(k == 0)
        def _():
            c_tgt.wait()

        err = recon + decb_v[:, pl.ds(pl.multiple_of(fea * blk, blk), blk)] - tgt[s].astype(F32)
        eall[s, pl.ds(0, blk)] = err.astype(BF)
        for p in range(1, NZ):
            send("ZA", k, eall.at[s, pl.ds(0, blk)], eall.at[s, pl.ds((NZ - p) * blk, blk)], dev(dzh=p))
        bsum[...] += fold(err)
        sq[...] += fold(err * err)

    def p8(k):
        s = span(k)
        got("ZA", k, eall.at[s, pl.ds(blk, 3 * blk)])
        send("XP", k, eall.at[s, pl.ds(0, group)], eall.at[s, pl.ds(3 * group, group)], dev(dx=1))
        send("XM", k, eall.at[s, pl.ds(0, group)], eall.at[s, pl.ds(group, group)], dev(dx=3))

    def p8a(k):
        s = span(k)
        got("XP", k, eall.at[s, pl.ds(3 * group, group)])
        send("FP", k, eall.at[s, pl.ds(3 * group, hg)], eall.at[s, pl.ds(2 * group, hg)], dev(dx=1))
        got("XM", k, eall.at[s, pl.ds(group, group)])
        send("FM", k, eall.at[s, pl.ds(group + hg, hg)], eall.at[s, pl.ds(2 * group + hg, hg)], dev(dx=3))

    def p9(k):
        s = span(k)
        got("FP", k, eall.at[s, pl.ds(2 * group, hg)])
        got("FM", k, eall.at[s, pl.ds(2 * group + hg, hg)])
        e = eall[s]
        b_send[s] = dot(e, w[pl.ds(feats, feats)], ((1,), (1,)))
        send("SB", k, b_send.at[s], b_recv.at[s], dev(dc=1))
        b_own[s] = dot(e, w[pl.ds(0, feats)], ((1,), (1,)))

    def p10(k):
        s = span(k)
        got("SB", k, b_recv.at[s])
        by[s] = (b_own[s] + b_recv[s]).astype(BF)
        for o in range(1, NY):
            send("YB", k, by.at[piece(k, (y + o) % NY)], ryb.at[k, o - 1], dev(dy=o))

    def p11(k):
        got("YB", k, ryb.at[k])
        me = piece(k, y)
        zs_b[k] = (
            b_own[me] + b_recv[me] + ryb[k, 0].astype(F32) + ryb[k, 1].astype(F32) + ryb[k, 2].astype(F32)
        )
        send("ZB", k, zs_b.at[k], zr_b.at[k], dev(dzl=1))

    def p12(k):
        got("ZB", k, zr_b.at[k])
        dpre = (zs_b[k] + zr_b[k]) * gpr[k]
        r = dall.at[piece(k, y)]
        dall[piece(k, y)] = dpre.astype(BF)
        for o in range(1, NY):
            send("YD", k, r, r, dev(dy=o))
        pb[...] += fold(dpre)

        @pl.when(k == nch - 1)
        def _():
            for o in range(1, NY):
                send1("GB", pb, rpb.at[o - 1], dev(dy=o))

    def p13(k):
        got("YD", k, dall.at[pl.ds(0, 3 * rows)])

    stages = dict(P1=p1, P2=p2, P3=p3, P4=p4, P5=p5, P6A=p6a, P6=p6, P7=p7, P8=p8, P8A=p8a, P9=p9, P10=p10, P11=p11, P12=p12, P13=p13)

    def grad(base, which):
        def body(n, _):
            at = pl.multiple_of(n * group, group)
            gd[pl.ds(base, feats), pl.ds(at, group)] = dot(
                acts[:, pl.ds(base, feats)], eall[:, pl.ds(at, group)], ((0,), (0,))
            ).astype(BF)
            for p in range(NZ):
                part = gd.at[pl.ds(base, feats), pl.ds(pl.multiple_of(at + p * blk, blk), blk)]
                where = gd_h.at[0, :, pl.ds(column(n, p, core), blk)]
                if which:
                    send1("GD", part, where, dev(dc=1))
                else:
                    pltpu.make_async_copy(part, where, lsem.at[4]).start()
            return 0

        lax.fori_loop(0, NX, body, 0)

    def l1():
        for o in range(1, NZ):
            send1("L1", sq, rl1.at[o - 1], dev(dzh=o))

    def l2():
        got1("L1", rl1)
        sl2[...] = sq[...] + rl1[0] + rl1[1] + rl1[2]
        for o in range(1, NX):
            send1("L2", sl2, rl2.at[o - 1], dev(dx=o))

    def l3():
        got1("L2", rl2)
        sl3[...] = sl2[...] + rl2[0] + rl2[1] + rl2[2]
        send1("L3", sl3, rl3, dev(dc=1))

    def l4():
        got1("L3", rl3)
        sl4[...] = sl3[...] + rl3[...]
        for o in range(1, NY):
            send1("L4", sl4, rl4.at[o - 1], dev(dy=o))

    def l5():
        got1("L4", rl4)
        sl5[...] = sl4[...] + rl4[0] + rl4[1] + rl4[2]
        send1("L5", sl5, rl5, dev(dzl=1))

    last = nch - 1
    extra = {
        "P7": [(LAG["P7"] + last, l1)],
        "P8": [(LAG["P8"] + last, l2)],
        "P8A": [(LAG["P8A"] + last, l3)],
        "P10": [(LAG["P10"] + last, lambda: grad(feats, True)), (LAG["P10"] + last, l4)],
        "P11": [(LAG["P11"] + last, lambda: grad(0, False)), (LAG["P11"] + last, l5)],
    }

    def iteration(t, _):
        for name in ORDER:
            k = t - LAG[name]

            @pl.when((k >= 0) & (k < nch))
            def _(name=name, k=k):
                stages[name](k)

            for when, what in extra.get(name, ()):
                pl.when(t == when)(what)
        return 0

    lax.fori_loop(0, max(LAG.values()) + nch, iteration, 0)

    ge_v[...] = dot(src[...], dall[...], ((0,), (0,)))
    got1("GB", rpb)
    geb_v[...] = jnp.sum(pb[...] + rpb[0] + rpb[1] + rpb[2], axis=0, keepdims=True)
    gdb_v[...] = jnp.sum(bsum[...], axis=0, keepdims=True)
    got1("L5", rl5)
    layers = 2 * NY
    width = 2 * half
    loss_s[0, 0] = jnp.sum(sl5[...] + rl5[...]) / (2.0 * tok * layers * width)

    own_gd = gd.at[pl.ds(0, feats)]
    pltpu.make_async_copy(own_gd, own_gd, lsem.at[4]).wait()
    got1("GD", own_gd)
    q3 = 3 * tok // 4
    left = dict(
        YR=ry, ZP=zr_p, YA=acts.at[pl.ds(0, q3), pl.ds(0, feats)], SA=acts.at[:, pl.ds(0, feats)], HP=hp, HM=hm, OP=op, OM=om,
        AP=ap, AM=am, ZR=rz, ZA=eall.at[:, pl.ds(0, 3 * blk)], XP=eall.at[:, pl.ds(0, group)], XM=eall.at[:, pl.ds(0, group)],
        FP=hp, FM=hm, SB=b_recv, YB=ryb, ZB=zr_b, YD=dall.at[pl.ds(0, q3)],
    )
    for name, ref in left.items():
        pltpu.make_async_copy(ref, ref, ssem.at[ID[name]]).wait()
    once = dict(W=w.at[pl.ds(0, feats)], GB=rpb, L1=rl1, L2=rl2, L3=rl3, L4=rl4, L5=rl5, GD=own_gd)
    for name, ref in once.items():
        pltpu.make_async_copy(ref, ref, oss.at[OID[name]]).wait()


def shards(source, enc_weight, enc_bias, dec_weight, dec_bias, target):
    tok, depth = source.shape
    feats = enc_weight.shape[1]
    width = dec_weight.shape[2]
    half = width // 2
    group = half // NX
    hg = group // 2
    blk = group // NZ
    nch = tok // CHUNK
    rows = CHUNK // NY
    V = pltpu.VMEM
    any_spec = pl.BlockSpec(memory_space=pl.ANY)
    vmem_spec = pl.BlockSpec(memory_space=pltpu.VMEM)
    scratch = [
        V((tok, depth), BF), V((depth, feats), BF), V((tok, blk), BF), V((2 * feats, half), BF),
        V((tok, feats), F32), V((nch, 3, rows, feats), F32), V((nch, rows, feats), F32), V((nch, rows, feats), F32),
        V((nch, rows, feats), F32), V((tok, 2 * feats), BF), V((tok, half), BF), V((tok, group), F32),
        V((tok, hg), BF), V((tok, hg), BF), V((tok, hg), BF), V((tok, hg), BF), V((tok, hg), BF), V((tok, hg), BF),
        V((tok, hg), BF), V((tok, hg), BF), V((tok, group), BF), V((tok, blk), F32), V((nch, 3, CHUNK, blk), BF), V((tok, half), BF),
        V((tok, feats), F32), V((tok, feats), F32), V((tok, feats), F32), V((tok, feats), BF), V((nch, 3, rows, feats), BF),
        V((nch, rows, feats), F32), V((nch, rows, feats), F32), V((tok, feats), BF), V((2 * feats, half), BF),
        V((8, feats), F32), V((3, 8, feats), F32), V((8, blk), F32), V((3, 8, blk), F32), V((3, 8, blk), F32), V((8, blk), F32),
        V((3, 8, blk), F32), V((8, blk), F32), V((8, blk), F32), V((8, blk), F32), V((8, blk), F32), V((8, blk), F32), V((8, blk), F32),
        pltpu.SemaphoreType.DMA((5,)), pltpu.SemaphoreType.DMA((len(KINDS),)), pltpu.SemaphoreType.DMA((len(KINDS), nch)),
        pltpu.SemaphoreType.DMA((len(ONCE),)), pltpu.SemaphoreType.DMA((len(ONCE),)),
    ]
    ge, geb, gd, gdb, loss = pl.pallas_call(
        kernel,
        out_shape=(
            jax.ShapeDtypeStruct((depth, feats), F32),
            jax.ShapeDtypeStruct((1, feats), F32),
            jax.ShapeDtypeStruct((1, feats, width), BF),
            jax.ShapeDtypeStruct((1, blk), F32),
            jax.ShapeDtypeStruct((1, 1), F32),
        ),
        in_specs=[any_spec, any_spec, vmem_spec, any_spec, vmem_spec, any_spec],
        out_specs=(vmem_spec, vmem_spec, any_spec, vmem_spec, pl.BlockSpec(memory_space=pltpu.SMEM)),
        scratch_shapes=scratch,
        compiler_params=pltpu.CompilerParams(collective_id=0, has_side_effects=True, vmem_limit_bytes=56 << 20),
    )(source, enc_weight, enc_bias.reshape(1, feats), dec_weight, dec_bias, target)
    return ge, geb.reshape(feats), gd, gdb, loss.reshape(())


def solution(mesh):
    return jax.shard_map(
        shards,
        mesh=mesh,
        in_specs=(
            P(None, "layer"),
            P("layer", "feat"),
            P("feat"),
            P("layer", "feat", None),
            P("layer", None),
            P("layer", None, None),
        ),
        out_specs=(
            P("layer", "feat"),
            P("feat"),
            P("layer", "feat", None),
            P("layer", "feat"),
            P(),
        ),
        check_vma=False,
    )
```

time: 551 us -> 120 us (0.22)
  waiting for transfers between devices: 411 us -> 0 us
  Pallas kernels: 0 us -> 107 us
  blocking collectives: 83.6 us -> 0 us
  matrix products: 24.6 us -> 0 us
  between operations: 15.6 us -> 2.38 us
  other arithmetic: 9.98 us -> 0 us
    psum x3 -> x0, waiting for transfers between devices: 411 us -> none  [the longest x1 330 us: shards(): recon = lax.psum(partial_rec, 'feat') + dec_bias[0]]
    pallas_call x0 -> x1, Pallas kernels: none -> 107 us  [shards(): pl.pallas_call(kernel, out_shape=(jax.ShapeDtypeStruct((depth, feats), F3...]
    psum x1 -> x0, blocking collectives: 83.6 us -> none  [shards(): squares = lax.psum(jnp.sum(err_own * err_own), ('layer', 'feat'))]
    dot_general x5 -> x0, matrix products: 24.6 us -> none  [the longest x1 8.24 us: shards(): partial_rec = jnp.dot(acts, weight, preferred_element_type=jnp.float32)]
    sub x1 -> x0, other arithmetic: 5.77 us -> none  [shards(): err = recon - target[0].astype(jnp.float32)]
  transfers between devices with their start and end apart: 3 -> 0, of which waited for: 2 -> 0; matrix products, arithmetic and copies ran while one was open for 2% -> 0% of each run, Pallas kernels for 0% -> 0%
where the time goes in v1:
time: 120 us; the launch traced here: 118 us
  Pallas kernels  107 us (89%)
  local copies, waits for them, and re-layouts  8.73 us (7%)
  between operations  2.38 us (2%)
    pallas_call x1, Pallas kernels, shards(): pl.pallas_call(kernel, out_shape=(jax.ShapeDtypeStruct((depth, feats), F3...  107 us
    unnamed x6, local copies, waits for them, and re-layouts  8.73 us

profile of v1, /device:TPU:1, one launch (start us, length us, event | category | flops | bytes accessed | tf_op | source)
XLA Modules:
  0.0 118.4 jit_solution(16548317377122826593)
XLA Ops:
  0.6 107.3 %shard_map.101 = (f32[512,512]{1,0:T(8,128)}, f32[1,512]{1,0:T(1,128)}, bf16[1,512,4096]{2,1,0:T(8,128)(2,1)}, f32[1,128]{1,0:T(1,128)}, f32[1,1]{1,0:T(1,128)}) custom-call(bf16[512,512]{1,0:T(8,128)(2,1)} %src_h.1, bf16[512,512]{1,0:T(8,128)(2,1)} %enc_h.1, f32[1,512]{1,0:T(1,128)} %bitcast.4, bf16[1,512,4096]{2,1,0:T(8,128)(2,1)} %w_h.1, ...), custom_call_target="tpu_custom_call" | custom-call | tf_op jit(solution)/shard_map/pallas_call | solution.py:378
  108.0 2.3 %copy.16 = f32[512,512]{1,0:T(8,128)} copy(f32[512,512]{1,0:T(8,128)} %get-tuple-element.20) | data formatting | bytes 2097152
  110.2 1.3 %copy.17 = f32[512]{0:T(512)} copy(f32[512]{0:T(512)} %bitcast.3) | data formatting | bytes 4096
  111.5 0.0 copy-start
  111.5 4.7 %copy.18 = bf16[1,512,4096]{2,1,0:T(8,128)(2,1)} copy(bf16[1,512,4096]{2,1,0:T(8,128)(2,1)} %get-tuple-element.22) | data formatting | bytes 8388608
  116.2 0.0 copy-done
  116.2 0.5 copy.19
Async XLA Ops:
  111.5 4.7 %copy-start = (f32[1,128]{1,0:T(1,128)S(1)}, f32[1,128]{1,0:T(1,128)}, u32[]{:S(2)}) copy-start(f32[1,128]{1,0:T(1,128)} %get-tuple-element.23) | copy-start | bytes 1540

commit v2 on v1

--- a/solution.py
+++ b/solution.py
@@ -13,9 +13,17 @@
 
 NY, NX, NZ = 4, 4, 4
 CHUNK = 64
-LAG = dict(P1=0, P2=1, P3=2, P4=3, P5=4, P6A=5, P6=6, P7=7, P8=8, P8A=9, P9=10, P10=11, P11=12, P12=13, P13=14)
-ORDER = ("P13", "P12", "P11", "P10", "P9", "P8A", "P8", "P7", "P6", "P6A", "P5", "P4", "P3", "P2", "P1")
-KINDS = ("YR", "ZP", "YA", "SA", "HP", "HM", "OP", "OM", "AP", "AM", "ZR", "ZA", "XP", "XM", "FP", "FM", "SB", "YB", "ZB", "YD")
+STAGES = ("P1", "P2", "P3", "P4", "P5", "P6A", "P6", "P7", "P8", "P8A", "P9", "P10", "P11", "P12")
+SCHEDULE = (
+    0, 1, 2, 3, 17, 32, 4, 18, 33, 5, 19, 48, 34, 6, 64, 20, 49, 35, 7, 65,
+    21, 50, 80, 36, 66, 22, 51, 81, 37, 96, 67, 23, 52, 82, 38, 97, 68, 53, 83, 39,
+    112, 98, 69, 54, 84, 113, 99, 70, 128, 55, 85, 114, 100, 71, 129, 144, 86, 115, 101, 130,
+    145, 87, 116, 160, 102, 131, 146, 176, 117, 161, 103, 132, 147, 177, 118, 162, 133, 148, 192, 178,
+    119, 163, 134, 149, 193, 179, 164, 208, 135, 150, 194, 180, 165, 209, 195, 181, 166, 210, 196, 182,
+    167, 211, 197, 183, 224, 225, 212, 198, 213, 214, 215,
+)
+PRE_DIRECT, BACK_DIRECT, X_DIRECT = (0,), (7,), (7,)
+KINDS = ("YR", "ZP", "YA", "SA", "HP", "HM", "OP", "OM", "AP", "AM", "ZR", "ZA", "XP", "XM", "FP", "FM", "SB", "YB", "ZB", "YD", "D1", "D2", "X2")
 ID = {name: i for i, name in enumerate(KINDS)}
 ONCE = ("W", "GB", "L1", "L2", "L3", "L4", "L5", "GD")
 OID = {name: i for i, name in enumerate(ONCE)}
@@ -28,10 +36,10 @@
 
 
 def kernel(
-    src_h, enc_h, encb_v, w_h, decb_v, tgt_h,
+    src_h, enc_h, encb_h, w_h, decb_h, tgt_h,
     ge_v, geb_v, gd_h, gdb_v, loss_s,
-    src, enc, tgt, w, ps, ry, zs_p, zr_p, gpr, acts, rec, own, hp, hm, op, om, ap, am, sp, sm, zsend, zown, rz, eall,
-    b_own, b_send, b_recv, by, ryb, zs_b, zr_b, dall, gd, pb, rpb, sq, rl1, rl2, rl3, rl4, rl5, sl2, sl3, sl4, sl5, bsum,
+    src, enc, tgt, encb_v, decb_v, w, ps, ry, zs_p, zr_p, gpr, acts, rec, own, hp, hm, op, om, ap, am, sp, sm, zsend, zown, rz, eall,
+    b_own, b_send, b_recv, by, ryb, zs_b, zr_b, dall, gd, pb, rpb, sq, rl1, rl2, rl3, rl4, rl5, sl2, sl3, sl4, sl5, bsum, psb, rd1, rd2,
     lsem, ssem, rsem, oss, ors,
 ):
     tok, depth = src.shape
@@ -71,7 +79,7 @@
 
     barrier = pltpu.get_barrier_semaphore()
     peers = (
-        [dict(dy=o) for o in range(1, NY)] + [dict(dzl=1), dict(dc=1)]
+        [dict(dzl=z, dy=o) for z in range(2) for o in range(NY) if z or o] + [dict(dc=1)]
         + [dict(dx=o) for o in range(1, NX)] + [dict(dzh=o) for o in range(1, NZ)]
     )
     for p in peers:
@@ -94,6 +102,14 @@
             ).start()
     c_tgt = pltpu.make_async_copy(tgt_h.at[0, :, pl.ds(pl.multiple_of(fea * blk, blk), blk)], tgt, lsem.at[3])
     c_tgt.start()
+    c_encb = pltpu.make_async_copy(encb_h, encb_v, lsem.at[5])
+    c_encb.start()
+    c_decb = pltpu.make_async_copy(decb_h.at[:, pl.ds(pl.multiple_of(fea * blk, blk), blk)], decb_v, lsem.at[6])
+    c_decb.start()
+    c_src.wait()
+    c_enc.wait()
+    c_encb.wait()
+    ps[...] = dot(src[...], enc[...], ((1,), (0,)))
     pl.semaphore_wait(barrier, len(peers))
     for o in range(NX):
         for p in range(NZ):
@@ -104,11 +120,9 @@
     sq[...] = jnp.zeros_like(sq)
     pb[...] = jnp.zeros_like(pb)
     bsum[...] = jnp.zeros_like(bsum)
-    c_src.wait()
-    c_enc.wait()
 
     def span(k):
-        return pl.ds(pl.multiple_of(k * tt, tt), tt)
+        return pl.ds(k * tt, tt)
 
     def piece(k, yy):
         return pl.ds(pl.multiple_of(k * tt + yy * rows, rows), rows)
@@ -116,8 +130,24 @@
     def fold(v):
         return jnp.sum(v.reshape(v.shape[0] // 8, 8, v.shape[1]), axis=0)
 
+    def everyone(kind, k, buf, slots):
+        slots[lay] = buf[piece(k, y)]
+        for dzl in range(2):
+            for o in range(NY):
+                if dzl or o:
+                    send(kind, k, buf.at[piece(k, (y + o) % NY)], slots.at[lay], dev(dzl=dzl, dy=o))
+
+    def total(slots):
+        v = slots[0].astype(F32)
+        for i in range(1, 2 * NY):
+            v = v + slots[i].astype(F32)
+        return v
+
     def p1(k):
-        ps[span(k)] = dot(src[span(k)], enc[...], ((1,), (0,)))
+        if k in PRE_DIRECT:
+            psb[span(k)] = ps[span(k)].astype(BF)
+            everyone("D1", k, psb, rd1.at[k])
+            return
         for o in range(1, NY):
             send("YR", k, ps.at[piece(k, (y + o) % NY)], ry.at[k, o - 1], dev(dy=o))
 
@@ -127,8 +157,12 @@
         send("ZP", k, zs_p.at[k], zr_p.at[k], dev(dzl=1))
 
     def p3(k):
-        got("ZP", k, zr_p.at[k])
-        v = zs_p[k] + zr_p[k] + encb_v[...]
+        if k in PRE_DIRECT:
+            got("D1", k, rd1.at[k, pl.ds(0, 2 * NY - 1)])
+            v = total(rd1.at[k]) + encb_v[...]
+        else:
+            got("ZP", k, zr_p.at[k])
+            v = zs_p[k] + zr_p[k] + encb_v[...]
         v2 = v * v
         t = jnp.tanh(A0 * (v * (1.0 + A1 * v2)))
         h = 0.5 * (1.0 + t)
@@ -145,8 +179,7 @@
     def p5(k):
         got("SA", k, acts.at[span(k), pl.ds(feats, feats)])
 
-        @pl.when(k == 0)
-        def _():
+        if k == 0:
             pltpu.make_async_copy(w.at[pl.ds(0, feats)], w.at[pl.ds(0, feats)], lsem.at[2]).wait()
             got1("W", w.at[pl.ds(feats, feats)])
 
@@ -191,11 +224,11 @@
         got("ZR", k, rz.at[k])
         recon = zown[s] + rz[k, 0].astype(F32) + rz[k, 1].astype(F32) + rz[k, 2].astype(F32)
 
-        @pl.when(k == 0)
-        def _():
+        if k == 0:
             c_tgt.wait()
-
-        err = recon + decb_v[:, pl.ds(pl.multiple_of(fea * blk, blk), blk)] - tgt[s].astype(F32)
+            c_decb.wait()
+
+        err = recon + decb_v[...] - tgt[s].astype(F32)
         eall[s, pl.ds(0, blk)] = err.astype(BF)
         for p in range(1, NZ):
             send("ZA", k, eall.at[s, pl.ds(0, blk)], eall.at[s, pl.ds((NZ - p) * blk, blk)], dev(dzh=p))
@@ -207,6 +240,8 @@
         got("ZA", k, eall.at[s, pl.ds(blk, 3 * blk)])
         send("XP", k, eall.at[s, pl.ds(0, group)], eall.at[s, pl.ds(3 * group, group)], dev(dx=1))
         send("XM", k, eall.at[s, pl.ds(0, group)], eall.at[s, pl.ds(group, group)], dev(dx=3))
+        if k in X_DIRECT:
+            send("X2", k, eall.at[s, pl.ds(0, group)], eall.at[s, pl.ds(2 * group, group)], dev(dx=2))
 
     def p8a(k):
         s = span(k)
@@ -217,8 +252,13 @@
 
     def p9(k):
         s = span(k)
-        got("FP", k, eall.at[s, pl.ds(2 * group, hg)])
-        got("FM", k, eall.at[s, pl.ds(2 * group + hg, hg)])
+        if k in X_DIRECT:
+            got("XP", k, eall.at[s, pl.ds(3 * group, group)])
+            got("XM", k, eall.at[s, pl.ds(group, group)])
+            got("X2", k, eall.at[s, pl.ds(2 * group, group)])
+        else:
+            got("FP", k, eall.at[s, pl.ds(2 * group, hg)])
+            got("FM", k, eall.at[s, pl.ds(2 * group + hg, hg)])
         e = eall[s]
         b_send[s] = dot(e, w[pl.ds(feats, feats)], ((1,), (1,)))
         send("SB", k, b_send.at[s], b_recv.at[s], dev(dc=1))
@@ -228,6 +268,9 @@
         s = span(k)
         got("SB", k, b_recv.at[s])
         by[s] = (b_own[s] + b_recv[s]).astype(BF)
+        if k in BACK_DIRECT:
+            everyone("D2", k, by, rd2.at[k])
+            return
         for o in range(1, NY):
             send("YB", k, by.at[piece(k, (y + o) % NY)], ryb.at[k, o - 1], dev(dy=o))
 
@@ -240,23 +283,26 @@
         send("ZB", k, zs_b.at[k], zr_b.at[k], dev(dzl=1))
 
     def p12(k):
-        got("ZB", k, zr_b.at[k])
-        dpre = (zs_b[k] + zr_b[k]) * gpr[k]
+        if k in BACK_DIRECT:
+            got("D2", k, rd2.at[k, pl.ds(0, 2 * NY - 1)])
+            dpre = total(rd2.at[k]) * gpr[k]
+        else:
+            got("ZB", k, zr_b.at[k])
+            dpre = (zs_b[k] + zr_b[k]) * gpr[k]
         r = dall.at[piece(k, y)]
         dall[piece(k, y)] = dpre.astype(BF)
         for o in range(1, NY):
             send("YD", k, r, r, dev(dy=o))
         pb[...] += fold(dpre)
 
-        @pl.when(k == nch - 1)
-        def _():
+        if k == nch - 1:
             for o in range(1, NY):
                 send1("GB", pb, rpb.at[o - 1], dev(dy=o))
 
     def p13(k):
         got("YD", k, dall.at[pl.ds(0, 3 * rows)])
 
-    stages = dict(P1=p1, P2=p2, P3=p3, P4=p4, P5=p5, P6A=p6a, P6=p6, P7=p7, P8=p8, P8A=p8a, P9=p9, P10=p10, P11=p11, P12=p12, P13=p13)
+    stages = dict(P1=p1, P2=p2, P3=p3, P4=p4, P5=p5, P6A=p6a, P6=p6, P7=p7, P8=p8, P8A=p8a, P9=p9, P10=p10, P11=p11, P12=p12)
 
     def grad(base, which):
         def body(n, _):
@@ -302,28 +348,19 @@
         send1("L5", sl5, rl5, dev(dzl=1))
 
     last = nch - 1
-    extra = {
-        "P7": [(LAG["P7"] + last, l1)],
-        "P8": [(LAG["P8"] + last, l2)],
-        "P8A": [(LAG["P8A"] + last, l3)],
-        "P10": [(LAG["P10"] + last, lambda: grad(feats, True)), (LAG["P10"] + last, l4)],
-        "P11": [(LAG["P11"] + last, lambda: grad(0, False)), (LAG["P11"] + last, l5)],
-    }
-
-    def iteration(t, _):
-        for name in ORDER:
-            k = t - LAG[name]
-
-            @pl.when((k >= 0) & (k < nch))
-            def _(name=name, k=k):
-                stages[name](k)
-
-            for when, what in extra.get(name, ()):
-                pl.when(t == when)(what)
-        return 0
-
-    lax.fori_loop(0, max(LAG.values()) + nch, iteration, 0)
-
+    side = {"P7": l1, "P8": l2, "P9": l3, "P10": l4, "P12": l5}
+    for code in SCHEDULE:
+        stage, k = code // 16, code % 16
+        if stage == len(STAGES):
+            grad(feats * (1 - k), k == 0)
+            continue
+        name = STAGES[stage]
+        stages[name](k)
+        if k == last and name in side:
+            side[name]()
+
+    for k in range(nch):
+        p13(k)
     ge_v[...] = dot(src[...], dall[...], ((0,), (0,)))
     got1("GB", rpb)
     geb_v[...] = jnp.sum(pb[...] + rpb[0] + rpb[1] + rpb[2], axis=0, keepdims=True)
@@ -336,17 +373,41 @@
     own_gd = gd.at[pl.ds(0, feats)]
     pltpu.make_async_copy(own_gd, own_gd, lsem.at[4]).wait()
     got1("GD", own_gd)
+    def drain(kind, ref, only=None, skip=()):
+        for k in range(nch) if only is None else only:
+            if k not in skip:
+                r = ref(k)
+                pltpu.make_async_copy(r, r, ssem.at[ID[kind]]).wait()
+
+    most = 2 * NY - 1
+    drain("YR", lambda k: ry.at[k], skip=PRE_DIRECT)
+    drain("ZP", lambda k: zr_p.at[k], skip=PRE_DIRECT)
+    drain("D1", lambda k: rd1.at[k, pl.ds(0, most)], only=PRE_DIRECT)
+    drain("YB", lambda k: ryb.at[k], skip=BACK_DIRECT)
+    drain("ZB", lambda k: zr_b.at[k], skip=BACK_DIRECT)
+    drain("D2", lambda k: rd2.at[k, pl.ds(0, most)], only=BACK_DIRECT)
+    drain("FP", lambda k: hp.at[span(k)], skip=X_DIRECT)
+    drain("FM", lambda k: hm.at[span(k)], skip=X_DIRECT)
+    drain("X2", lambda k: eall.at[span(k), pl.ds(0, group)], only=X_DIRECT)
     q3 = 3 * tok // 4
     left = dict(
-        YR=ry, ZP=zr_p, YA=acts.at[pl.ds(0, q3), pl.ds(0, feats)], SA=acts.at[:, pl.ds(0, feats)], HP=hp, HM=hm, OP=op, OM=om,
-        AP=ap, AM=am, ZR=rz, ZA=eall.at[:, pl.ds(0, 3 * blk)], XP=eall.at[:, pl.ds(0, group)], XM=eall.at[:, pl.ds(0, group)],
-        FP=hp, FM=hm, SB=b_recv, YB=ryb, ZB=zr_b, YD=dall.at[pl.ds(0, q3)],
+        YA=acts.at[pl.ds(0, q3), pl.ds(0, feats)], SA=acts.at[:, pl.ds(0, feats)], HP=hp, HM=hm, OP=op, OM=om, AP=ap, AM=am,
+        ZR=rz, ZA=eall.at[:, pl.ds(0, 3 * blk)], XP=eall.at[:, pl.ds(0, group)], XM=eall.at[:, pl.ds(0, group)], SB=b_recv,
+        YD=dall.at[pl.ds(0, q3)],
     )
     for name, ref in left.items():
         pltpu.make_async_copy(ref, ref, ssem.at[ID[name]]).wait()
     once = dict(W=w.at[pl.ds(0, feats)], GB=rpb, L1=rl1, L2=rl2, L3=rl3, L4=rl4, L5=rl5, GD=own_gd)
     for name, ref in once.items():
         pltpu.make_async_copy(ref, ref, oss.at[OID[name]]).wait()
+
+
+def place(a, b, c, d, ao, bo, co, do, sem):
+    copies = [pltpu.make_async_copy(i, o, sem.at[n]) for n, (i, o) in enumerate(((a, ao), (b, bo), (c, co), (d, do)))]
+    for copy in copies:
+        copy.start()
+    for copy in copies:
+        copy.wait()
 
 
 def shards(source, enc_weight, enc_bias, dec_weight, dec_bias, target):
@@ -361,9 +422,10 @@
     rows = CHUNK // NY
     V = pltpu.VMEM
     any_spec = pl.BlockSpec(memory_space=pl.ANY)
+    hbm_spec = pl.BlockSpec(memory_space=pltpu.HBM)
     vmem_spec = pl.BlockSpec(memory_space=pltpu.VMEM)
     scratch = [
-        V((tok, depth), BF), V((depth, feats), BF), V((tok, blk), BF), V((2 * feats, half), BF),
+        V((tok, depth), BF), V((depth, feats), BF), V((tok, blk), BF), V((1, feats), F32), V((1, blk), F32), V((2 * feats, half), BF),
         V((tok, feats), F32), V((nch, 3, rows, feats), F32), V((nch, rows, feats), F32), V((nch, rows, feats), F32),
         V((nch, rows, feats), F32), V((tok, 2 * feats), BF), V((tok, half), BF), V((tok, group), F32),
         V((tok, hg), BF), V((tok, hg), BF), V((tok, hg), BF), V((tok, hg), BF), V((tok, hg), BF), V((tok, hg), BF),
@@ -372,7 +434,8 @@
         V((nch, rows, feats), F32), V((nch, rows, feats), F32), V((tok, feats), BF), V((2 * feats, half), BF),
         V((8, feats), F32), V((3, 8, feats), F32), V((8, blk), F32), V((3, 8, blk), F32), V((3, 8, blk), F32), V((8, blk), F32),
         V((3, 8, blk), F32), V((8, blk), F32), V((8, blk), F32), V((8, blk), F32), V((8, blk), F32), V((8, blk), F32), V((8, blk), F32),
-        pltpu.SemaphoreType.DMA((5,)), pltpu.SemaphoreType.DMA((len(KINDS),)), pltpu.SemaphoreType.DMA((len(KINDS), nch)),
+        V((tok, feats), BF), V((nch, 2 * NY, rows, feats), BF), V((nch, 2 * NY, rows, feats), BF),
+        pltpu.SemaphoreType.DMA((7,)), pltpu.SemaphoreType.DMA((len(KINDS),)), pltpu.SemaphoreType.DMA((len(KINDS), nch)),
         pltpu.SemaphoreType.DMA((len(ONCE),)), pltpu.SemaphoreType.DMA((len(ONCE),)),
     ]
     ge, geb, gd, gdb, loss = pl.pallas_call(
@@ -384,11 +447,20 @@
             jax.ShapeDtypeStruct((1, blk), F32),
             jax.ShapeDtypeStruct((1, 1), F32),
         ),
-        in_specs=[any_spec, any_spec, vmem_spec, any_spec, vmem_spec, any_spec],
+        in_specs=[any_spec] * 6,
         out_specs=(vmem_spec, vmem_spec, any_spec, vmem_spec, pl.BlockSpec(memory_space=pltpu.SMEM)),
         scratch_shapes=scratch,
-        compiler_params=pltpu.CompilerParams(collective_id=0, has_side_effects=True, vmem_limit_bytes=56 << 20),
-    )(source, enc_weight, enc_bias.reshape(1, feats), dec_weight, dec_bias, target)
+        compiler_params=pltpu.CompilerParams(collective_id=0, has_side_effects=True, vmem_limit_bytes=45 << 20),
+    )(*(pltpu.with_memory_space_constraint(v, pltpu.HBM) for v in (source, enc_weight, enc_bias.reshape(1, feats), dec_weight, dec_bias, target)))
+    outs = (ge, geb, gd, gdb)
+    ge, geb, gd, gdb = pl.pallas_call(
+        place,
+        out_shape=tuple(pltpu.HBM(v.shape, v.dtype) for v in outs),
+        in_specs=[any_spec] * 4,
+        out_specs=(any_spec,) * 4,
+        scratch_shapes=[pltpu.SemaphoreType.DMA((4,))],
+        compiler_params=pltpu.CompilerParams(vmem_limit_bytes=1 << 20),
+    )(*(pltpu.with_memory_space_constraint(v, pltpu.VMEM) for v in outs))
     return ge, geb.reshape(feats), gd, gdb, loss.reshape(())
 
 

time: 120 us -> 92.4 us (0.77); the launches traced: 118 us -> 92.3 us
  Pallas kernels: 107 us -> 89.9 us
  local copies, waits for them, and re-layouts: 8.73 us -> 0 us
    pallas_call x1, Pallas kernels: 107 us -> 87.5 us  [shards(): pl.pallas_call(kernel, out_shape=(jax.ShapeDtypeStruct((depth, feats), F3...]
    unnamed x6 -> x0, local copies, waits for them, and re-layouts: 8.73 us -> none
    pallas_call x0 -> x1, Pallas kernels: none -> 2.4 us  [shards(): pl.pallas_call(place, out_shape=tuple((pltpu.HBM(v.shape, v.dtype) for v...]
where the time goes in v2:
time: 92.4 us; the launch traced here: 92.3 us
  Pallas kernels  89.9 us (97%)
  between operations  2.41 us (3%)
    pallas_call x1, Pallas kernels, shards(): pl.pallas_call(kernel, out_shape=(jax.ShapeDtypeStruct((depth, feats), F3...  87.5 us
    pallas_call x1, Pallas kernels, shards(): pl.pallas_call(place, out_shape=tuple((pltpu.HBM(v.shape, v.dtype) for v...  2.4 us

profile of v2, /device:TPU:1, one launch (start us, length us, event | category | flops | bytes accessed | tf_op | source)
XLA Modules:
  0.0 92.3 jit_solution(3145430570912509578)
XLA Ops:
  0.6 87.5 %shard_map.101 = (f32[512,512]{1,0:T(8,128)S(1)}, f32[1,512]{1,0:T(1,128)S(1)}, bf16[1,512,4096]{2,1,0:T(8,128)(2,1)S(1)}, f32[1,128]{1,0:T(1,128)S(1)}, f32[1,1]{1,0:T(1,128)}) custom-call(bf16[512,512]{1,0:T(8,128)(2,1)} %src_h.1, bf16[512,512]{1,0:T(8,128)(2,1)} %enc_h.1, f32[1,512]{1,0:T(1,128)} %bitcast.3, bf16[1,512,4096]{2,1,0:T(8,128)(2,1)} %w_h.1, ...), custom_call_target="tpu_custom_call" | custom-call | tf_op jit(solution)/shard_map/pallas_call | solution.py:441
  88.1 2.4 %shard_map.102 = (f32[512,512]{1,0:T(8,128)}, f32[1,512]{1,0:T(1,128)}, bf16[1,512,4096]{2,1,0:T(8,128)(2,1)}, f32[1,128]{1,0:T(1,128)}) custom-call(f32[512,512]{1,0:T(8,128)S(1)} %get-tuple-element.14.a, f32[1,512]{1,0:T(1,128)S(1)} %get-tuple-element.15.b, bf16[1,512,4096]{2,1,0:T(8,128)(2,1)S(1)} %get-tuple-element.16.c, f32[1,128]{1,0:T(1,128)S(1)} %get-tuple-element.17.d), custom_call_target="tpu_custom_call" | custom-call | tf_op jit(solution)/shard_map/pallas_call | solution.py:456

commit v3 on v2

--- a/solution.py
+++ b/solution.py
@@ -15,12 +15,12 @@
 CHUNK = 64
 STAGES = ("P1", "P2", "P3", "P4", "P5", "P6A", "P6", "P7", "P8", "P8A", "P9", "P10", "P11", "P12")
 SCHEDULE = (
-    0, 1, 2, 3, 17, 32, 4, 18, 33, 5, 19, 48, 34, 6, 64, 20, 49, 35, 7, 65,
-    21, 50, 80, 36, 66, 22, 51, 81, 37, 96, 67, 23, 52, 82, 38, 97, 68, 53, 83, 39,
-    112, 98, 69, 54, 84, 113, 99, 70, 128, 55, 85, 114, 100, 71, 129, 144, 86, 115, 101, 130,
-    145, 87, 116, 160, 102, 131, 146, 176, 117, 161, 103, 132, 147, 177, 118, 162, 133, 148, 192, 178,
-    119, 163, 134, 149, 193, 179, 164, 208, 135, 150, 194, 180, 165, 209, 195, 181, 166, 210, 196, 182,
-    167, 211, 197, 183, 224, 225, 212, 198, 213, 214, 215,
+    2, 0, 1, 18, 5, 32, 17, 34, 3, 48, 6, 21, 33, 64, 50, 37, 19, 4, 66, 49,
+    22, 80, 7, 35, 65, 53, 82, 20, 38, 96, 69, 23, 81, 51, 36, 98, 67, 54, 85, 39,
+    97, 52, 112, 70, 83, 101, 114, 55, 68, 86, 113, 71, 99, 84, 128, 102, 117, 130, 87, 100,
+    144, 115, 129, 146, 103, 133, 118, 160, 145, 116, 131, 162, 149, 176, 119, 134, 161, 147, 178, 132,
+    165, 192, 150, 177, 181, 135, 163, 194, 148, 208, 166, 179, 197, 193, 210, 182, 164, 167, 180, 195,
+    213, 198, 183, 224, 196, 209, 211, 214, 215, 212, 225,
 )
 PRE_DIRECT, BACK_DIRECT, X_DIRECT = (0,), (7,), (7,)
 KINDS = ("YR", "ZP", "YA", "SA", "HP", "HM", "OP", "OM", "AP", "AM", "ZR", "ZA", "XP", "XM", "FP", "FM", "SB", "YB", "ZB", "YD", "D1", "D2", "X2")
@@ -295,9 +295,6 @@
             send("YD", k, r, r, dev(dy=o))
         pb[...] += fold(dpre)
 
-        if k == nch - 1:
-            for o in range(1, NY):
-                send1("GB", pb, rpb.at[o - 1], dev(dy=o))
 
     def p13(k):
         got("YD", k, dall.at[pl.ds(0, 3 * rows)])
@@ -321,6 +318,10 @@
 
         lax.fori_loop(0, NX, body, 0)
 
+    def bias():
+        for o in range(1, NY):
+            send1("GB", pb, rpb.at[o - 1], dev(dy=o))
+
     def l1():
         for o in range(1, NZ):
             send1("L1", sq, rl1.at[o - 1], dev(dzh=o))
@@ -347,8 +348,8 @@
         sl5[...] = sl4[...] + rl4[0] + rl4[1] + rl4[2]
         send1("L5", sl5, rl5, dev(dzl=1))
 
-    last = nch - 1
-    side = {"P7": l1, "P8": l2, "P9": l3, "P10": l4, "P12": l5}
+    side = {"P7": (l1,), "P8": (l2,), "P9": (l3,), "P10": (l4,), "P12": (bias, l5)}
+    left_of = [sum(c // 16 == i for c in SCHEDULE) for i in range(len(STAGES) + 1)]
     for code in SCHEDULE:
         stage, k = code // 16, code % 16
         if stage == len(STAGES):
@@ -356,8 +357,10 @@
             continue
         name = STAGES[stage]
         stages[name](k)
-        if k == last and name in side:
-            side[name]()
+        left_of[stage] -= 1
+        if left_of[stage] == 0:
+            for step in side.get(name, ()):
+                step()
 
     for k in range(nch):
         p13(k)

time: 92.4 us -> 87.7 us (0.949)
  Pallas kernels: 89.9 us -> 85.1 us
    pallas_call x1, Pallas kernels: 87.5 us -> 82.7 us  [shards(): pl.pallas_call(kernel, out_shape=(jax.ShapeDtypeStruct((depth, feats), F3...]
where the time goes in v3:
time: 87.7 us; the launch traced here: 87.6 us
  Pallas kernels  85.1 us (97%)
  between operations  2.41 us (3%)
    pallas_call x1, Pallas kernels, shards(): pl.pallas_call(kernel, out_shape=(jax.ShapeDtypeStruct((depth, feats), F3...  82.7 us
    pallas_call x1, Pallas kernels, shards(): pl.pallas_call(place, out_shape=tuple((pltpu.HBM(v.shape, v.dtype) for v...  2.4 us

profile of v3, /device:TPU:1, one launch (start us, length us, event | category | flops | bytes accessed | tf_op | source)
XLA Modules:
  0.0 87.6 jit_solution(14508435472754871119)
XLA Ops:
  0.6 82.7 %shard_map.101 = (f32[512,512]{1,0:T(8,128)S(1)}, f32[1,512]{1,0:T(1,128)S(1)}, bf16[1,512,4096]{2,1,0:T(8,128)(2,1)S(1)}, f32[1,128]{1,0:T(1,128)S(1)}, f32[1,1]{1,0:T(1,128)}) custom-call(bf16[512,512]{1,0:T(8,128)(2,1)} %src_h.1, bf16[512,512]{1,0:T(8,128)(2,1)} %enc_h.1, f32[1,512]{1,0:T(1,128)} %bitcast.3, bf16[1,512,4096]{2,1,0:T(8,128)(2,1)} %w_h.1, ...), custom_call_target="tpu_custom_call" | custom-call | tf_op jit(solution)/shard_map/pallas_call | solution.py:444
  83.4 2.4 %shard_map.102 = (f32[512,512]{1,0:T(8,128)}, f32[1,512]{1,0:T(1,128)}, bf16[1,512,4096]{2,1,0:T(8,128)(2,1)}, f32[1,128]{1,0:T(1,128)}) custom-call(f32[512,512]{1,0:T(8,128)S(1)} %get-tuple-element.14.a, f32[1,512]{1,0:T(1,128)S(1)} %get-tuple-element.15.b, bf16[1,512,4096]{2,1,0:T(8,128)(2,1)S(1)} %get-tuple-element.16.c, f32[1,128]{1,0:T(1,128)S(1)} %get-tuple-element.17.d), custom_call_target="tpu_custom_call" | custom-call | tf_op jit(solution)/shard_map/pallas_call | solution.py:459

commit v4 on v3

--- a/solution.py
+++ b/solution.py
@@ -15,14 +15,14 @@
 CHUNK = 64
 STAGES = ("P1", "P2", "P3", "P4", "P5", "P6A", "P6", "P7", "P8", "P8A", "P9", "P10", "P11", "P12")
 SCHEDULE = (
-    2, 0, 1, 18, 5, 32, 17, 34, 3, 48, 6, 21, 33, 64, 50, 37, 19, 4, 66, 49,
-    22, 80, 7, 35, 65, 53, 82, 20, 38, 96, 69, 23, 81, 51, 36, 98, 67, 54, 85, 39,
-    97, 52, 112, 70, 83, 101, 114, 55, 68, 86, 113, 71, 99, 84, 128, 102, 117, 130, 87, 100,
-    144, 115, 129, 146, 103, 133, 118, 160, 145, 116, 131, 162, 149, 176, 119, 134, 161, 147, 178, 132,
-    165, 192, 150, 177, 181, 135, 163, 194, 148, 208, 166, 179, 197, 193, 210, 182, 164, 167, 180, 195,
-    213, 198, 183, 224, 196, 209, 211, 214, 215, 212, 225,
+    6, 0, 5, 3, 22, 1, 21, 32, 38, 19, 37, 4, 48, 17, 54, 7, 35, 64, 2, 53,
+    70, 20, 69, 80, 51, 33, 23, 86, 36, 18, 67, 96, 49, 85, 34, 102, 52, 83, 39, 65,
+    101, 68, 112, 50, 55, 81, 99, 66, 118, 71, 117, 84, 97, 82, 128, 115, 100, 134, 87, 98,
+    133, 113, 144, 103, 150, 131, 116, 160, 149, 114, 129, 166, 119, 147, 176, 132, 165, 182, 145, 130,
+    192, 135, 181, 163, 198, 148, 161, 146, 208, 179, 151, 177, 197, 164, 214, 162, 180, 167, 195, 178,
+    193, 183, 224, 196, 213, 211, 194, 209, 215, 212, 210, 225,
 )
-PRE_DIRECT, BACK_DIRECT, X_DIRECT = (0,), (7,), (7,)
+PRE_DIRECT, BACK_DIRECT, X_DIRECT = (0,), (7,), ()
 KINDS = ("YR", "ZP", "YA", "SA", "HP", "HM", "OP", "OM", "AP", "AM", "ZR", "ZA", "XP", "XM", "FP", "FM", "SB", "YB", "ZB", "YD", "D1", "D2", "X2")
 ID = {name: i for i, name in enumerate(KINDS)}
 ONCE = ("W", "GB", "L1", "L2", "L3", "L4", "L5", "GD")
@@ -39,7 +39,7 @@
     src_h, enc_h, encb_h, w_h, decb_h, tgt_h,
     ge_v, geb_v, gd_h, gdb_v, loss_s,
     src, enc, tgt, encb_v, decb_v, w, ps, ry, zs_p, zr_p, gpr, acts, rec, own, hp, hm, op, om, ap, am, sp, sm, zsend, zown, rz, eall,
-    b_own, b_send, b_recv, by, ryb, zs_b, zr_b, dall, gd, pb, rpb, sq, rl1, rl2, rl3, rl4, rl5, sl2, sl3, sl4, sl5, bsum, psb, rd1, rd2,
+    b_own, b_send, b_recv, by, ryb, zs_b, zr_b, dall, gd, pb, rpb, sq, rl1, rl2, rl3, rl4, rl5, sl2, sl3, sl4, sl5, bsum, psb, rd1, rd2, wt,
     lsem, ssem, rsem, oss, ors,
 ):
     tok, depth = src.shape
@@ -110,16 +110,25 @@
     c_enc.wait()
     c_encb.wait()
     ps[...] = dot(src[...], enc[...], ((1,), (0,)))
+    for k in PRE_DIRECT:
+        psb[pl.ds(k * tt, tt)] = ps[pl.ds(k * tt, tt)].astype(BF)
     pl.semaphore_wait(barrier, len(peers))
-    for o in range(NX):
-        for p in range(NZ):
-            send1(
-                "W", w_h.at[0, :, pl.ds(column(o, p, 1 - core), blk)],
-                w.at[pl.ds(feats, feats), pl.ds((o * NZ + p) * blk, blk)], dev(dc=1),
-            )
     sq[...] = jnp.zeros_like(sq)
     pb[...] = jnp.zeros_like(pb)
     bsum[...] = jnp.zeros_like(bsum)
+
+    def swap():
+        for o in range(NX):
+            for p in range(NZ):
+                send1(
+                    "W", w_h.at[0, :, pl.ds(column(o, p, 1 - core), blk)],
+                    w.at[pl.ds(feats, feats), pl.ds((o * NZ + p) * blk, blk)], dev(dc=1),
+                )
+
+    last_p9 = [c % 16 for c in SCHEDULE if c // 16 == STAGES.index("P9")][-1]
+    last_p12 = [c % 16 for c in SCHEDULE if c // 16 == STAGES.index("P12")][-1]
+    b_send[pl.ds(last_p9 * tt, tt)] = jnp.zeros((tt, feats), F32)
+    b_own[pl.ds(last_p9 * tt, tt)] = jnp.zeros((tt, feats), F32)
 
     def span(k):
         return pl.ds(k * tt, tt)
@@ -145,7 +154,6 @@
 
     def p1(k):
         if k in PRE_DIRECT:
-            psb[span(k)] = ps[span(k)].astype(BF)
             everyone("D1", k, psb, rd1.at[k])
             return
         for o in range(1, NY):
@@ -252,17 +260,29 @@
 
     def p9(k):
         s = span(k)
+        late = k == last_p9
         if k in X_DIRECT:
             got("XP", k, eall.at[s, pl.ds(3 * group, group)])
             got("XM", k, eall.at[s, pl.ds(group, group)])
+        if late:
+            for c in (pl.ds(0, 2 * group), pl.ds(3 * group, group)):
+                b_send[s] += dot(eall[s, c], wt[c, pl.ds(feats, feats)], ((1,), (0,)))
+                b_own[s] += dot(eall[s, c], wt[c, pl.ds(0, feats)], ((1,), (0,)))
+        if k in X_DIRECT:
             got("X2", k, eall.at[s, pl.ds(2 * group, group)])
         else:
             got("FP", k, eall.at[s, pl.ds(2 * group, hg)])
             got("FM", k, eall.at[s, pl.ds(2 * group + hg, hg)])
-        e = eall[s]
-        b_send[s] = dot(e, w[pl.ds(feats, feats)], ((1,), (1,)))
-        send("SB", k, b_send.at[s], b_recv.at[s], dev(dc=1))
-        b_own[s] = dot(e, w[pl.ds(0, feats)], ((1,), (1,)))
+        if late:
+            c = pl.ds(2 * group, group)
+            b_send[s] += dot(eall[s, c], wt[c, pl.ds(feats, feats)], ((1,), (0,)))
+            send("SB", k, b_send.at[s], b_recv.at[s], dev(dc=1))
+            b_own[s] += dot(eall[s, c], wt[c, pl.ds(0, feats)], ((1,), (0,)))
+        else:
+            e = eall[s]
+            b_send[s] = dot(e, wt[:, pl.ds(feats, feats)], ((1,), (0,)))
+            send("SB", k, b_send.at[s], b_recv.at[s], dev(dc=1))
+            b_own[s] = dot(e, wt[:, pl.ds(0, feats)], ((1,), (0,)))
 
     def p10(k):
         s = span(k)
@@ -350,32 +370,29 @@
 
     side = {"P7": (l1,), "P8": (l2,), "P9": (l3,), "P10": (l4,), "P12": (bias, l5)}
     left_of = [sum(c // 16 == i for c in SCHEDULE) for i in range(len(STAGES) + 1)]
-    for code in SCHEDULE:
+    for at, code in enumerate(SCHEDULE):
+        if at == 0:
+            swap()
         stage, k = code // 16, code % 16
         if stage == len(STAGES):
             grad(feats * (1 - k), k == 0)
             continue
         name = STAGES[stage]
         stages[name](k)
+        seen = left_of[4]
         left_of[stage] -= 1
+        if name == "P5" and nch - NX - 1 < seen <= nch - 1:
+            q = pl.ds((nch - 1 - seen) * group, group)
+            wt[q, :] = w[:, q].T
         if left_of[stage] == 0:
             for step in side.get(name, ()):
                 step()
 
+    gdb_v[...] = jnp.sum(bsum[...], axis=0, keepdims=True)
     for k in range(nch):
-        p13(k)
-    ge_v[...] = dot(src[...], dall[...], ((0,), (0,)))
-    got1("GB", rpb)
-    geb_v[...] = jnp.sum(pb[...] + rpb[0] + rpb[1] + rpb[2], axis=0, keepdims=True)
-    gdb_v[...] = jnp.sum(bsum[...], axis=0, keepdims=True)
-    got1("L5", rl5)
-    layers = 2 * NY
-    width = 2 * half
-    loss_s[0, 0] = jnp.sum(sl5[...] + rl5[...]) / (2.0 * tok * layers * width)
-
-    own_gd = gd.at[pl.ds(0, feats)]
-    pltpu.make_async_copy(own_gd, own_gd, lsem.at[4]).wait()
-    got1("GD", own_gd)
+        if k != last_p12:
+            p13(k)
+
     def drain(kind, ref, only=None, skip=()):
         for k in range(nch) if only is None else only:
             if k not in skip:
@@ -396,17 +413,37 @@
     left = dict(
         YA=acts.at[pl.ds(0, q3), pl.ds(0, feats)], SA=acts.at[:, pl.ds(0, feats)], HP=hp, HM=hm, OP=op, OM=om, AP=ap, AM=am,
         ZR=rz, ZA=eall.at[:, pl.ds(0, 3 * blk)], XP=eall.at[:, pl.ds(0, group)], XM=eall.at[:, pl.ds(0, group)], SB=b_recv,
-        YD=dall.at[pl.ds(0, q3)],
     )
     for name, ref in left.items():
         pltpu.make_async_copy(ref, ref, ssem.at[ID[name]]).wait()
-    once = dict(W=w.at[pl.ds(0, feats)], GB=rpb, L1=rl1, L2=rl2, L3=rl3, L4=rl4, L5=rl5, GD=own_gd)
+    once = dict(W=w.at[pl.ds(0, feats)], L1=rl1, L2=rl2, L3=rl3, L4=rl4)
     for name, ref in once.items():
         pltpu.make_async_copy(ref, ref, oss.at[OID[name]]).wait()
+    own_gd = gd.at[pl.ds(0, feats)]
+    pltpu.make_async_copy(own_gd, own_gd, lsem.at[4]).wait()
+    got1("L5", rl5)
+    loss_s[0, 0] = jnp.sum(sl5[...] + rl5[...]) / (2.0 * tok * (2 * NY) * (2 * half))
+
+    p13(last_p12)
+    ge_v[...] = dot(src[...], dall[...], ((0,), (0,)))
+    got1("GB", rpb)
+    geb_v[...] = jnp.sum(pb[...] + rpb[0] + rpb[1] + rpb[2], axis=0, keepdims=True)
+    got1("GD", own_gd)
+    r = dall.at[pl.ds(0, q3)]
+    pltpu.make_async_copy(r, r, ssem.at[ID["YD"]]).wait()
+    for name, ref in dict(GB=rpb, L5=rl5, GD=own_gd).items():
+        pltpu.make_async_copy(ref, ref, oss.at[OID[name]]).wait()
 
 
 def place(a, b, c, d, ao, bo, co, do, sem):
-    copies = [pltpu.make_async_copy(i, o, sem.at[n]) for n, (i, o) in enumerate(((a, ao), (b, bo), (c, co), (d, do)))]
+    parts = [(b, bo), (d, do)]
+    for i in range(4):
+        r = pl.ds(i * (c.shape[1] // 4), c.shape[1] // 4)
+        parts.append((c.at[:, r], co.at[:, r]))
+    for i in range(2):
+        r = pl.ds(i * (a.shape[0] // 2), a.shape[0] // 2)
+        parts.append((a.at[r], ao.at[r]))
+    copies = [pltpu.make_async_copy(i, o, sem.at[n]) for n, (i, o) in enumerate(parts)]
     for copy in copies:
         copy.start()
     for copy in copies:
@@ -437,7 +474,7 @@
         V((nch, rows, feats), F32), V((nch, rows, feats), F32), V((tok, feats), BF), V((2 * feats, half), BF),
         V((8, feats), F32), V((3, 8, feats), F32), V((8, blk), F32), V((3, 8, blk), F32), V((3, 8, blk), F32), V((8, blk), F32),
         V((3, 8, blk), F32), V((8, blk), F32), V((8, blk), F32), V((8, blk), F32), V((8, blk), F32), V((8, blk), F32), V((8, blk), F32),
-        V((tok, feats), BF), V((nch, 2 * NY, rows, feats), BF), V((nch, 2 * NY, rows, feats), BF),
+        V((tok, feats), BF), V((nch, 2 * NY, rows, feats), BF), V((nch, 2 * NY, rows, feats), BF), V((half, 2 * feats), BF),
         pltpu.SemaphoreType.DMA((7,)), pltpu.SemaphoreType.DMA((len(KINDS),)), pltpu.SemaphoreType.DMA((len(KINDS), nch)),
         pltpu.SemaphoreType.DMA((len(ONCE),)), pltpu.SemaphoreType.DMA((len(ONCE),)),
     ]
@@ -461,7 +498,7 @@
         out_shape=tuple(pltpu.HBM(v.shape, v.dtype) for v in outs),
         in_specs=[any_spec] * 4,
         out_specs=(any_spec,) * 4,
-        scratch_shapes=[pltpu.SemaphoreType.DMA((4,))],
+        scratch_shapes=[pltpu.SemaphoreType.DMA((8,))],
         compiler_params=pltpu.CompilerParams(vmem_limit_bytes=1 << 20),
     )(*(pltpu.with_memory_space_constraint(v, pltpu.VMEM) for v in outs))
     return ge, geb.reshape(feats), gd, gdb, loss.reshape(())

time: 87.7 us -> 86.3 us (0.984)
  Pallas kernels: 85.1 us -> 83.7 us
    pallas_call x1, Pallas kernels: 82.7 us -> 81.3 us  [shards(): pl.pallas_call(kernel, out_shape=(jax.ShapeDtypeStruct((depth, feats), F3...]
where the time goes in v4:
time: 86.3 us; the launch traced here: 86.1 us
  Pallas kernels  83.7 us (97%)
  between operations  2.41 us (3%)
    pallas_call x1, Pallas kernels, shards(): pl.pallas_call(kernel, out_shape=(jax.ShapeDtypeStruct((depth, feats), F3...  81.3 us
    pallas_call x1, Pallas kernels, shards(): pl.pallas_call(place, out_shape=tuple((pltpu.HBM(v.shape, v.dtype) for v...  2.41 us

profile of v4, /device:TPU:1, one launch (start us, length us, event | category | flops | bytes accessed | tf_op | source)
XLA Modules:
  0.0 86.1 jit_solution(16311006366006726125)
XLA Ops:
  0.6 81.3 %shard_map.101 = (f32[512,512]{1,0:T(8,128)S(1)}, f32[1,512]{1,0:T(1,128)S(1)}, bf16[1,512,4096]{2,1,0:T(8,128)(2,1)S(1)}, f32[1,128]{1,0:T(1,128)S(1)}, f32[1,1]{1,0:T(1,128)}) custom-call(bf16[512,512]{1,0:T(8,128)(2,1)} %src_h.1, bf16[512,512]{1,0:T(8,128)(2,1)} %enc_h.1, f32[1,512]{1,0:T(1,128)} %bitcast.3, bf16[1,512,4096]{2,1,0:T(8,128)(2,1)} %w_h.1, ...), custom_call_target="tpu_custom_call" | custom-call | tf_op jit(solution)/shard_map/pallas_call | solution.py:481
  82.0 2.4 %shard_map.102 = (f32[512,512]{1,0:T(8,128)}, f32[1,512]{1,0:T(1,128)}, bf16[1,512,4096]{2,1,0:T(8,128)(2,1)}, f32[1,128]{1,0:T(1,128)}) custom-call(f32[512,512]{1,0:T(8,128)S(1)} %get-tuple-element.14.a, f32[1,512]{1,0:T(1,128)S(1)} %get-tuple-element.15.b, bf16[1,512,4096]{2,1,0:T(8,128)(2,1)S(1)} %get-tuple-element.16.c, f32[1,128]{1,0:T(1,128)S(1)} %get-tuple-element.17.d), custom_call_target="tpu_custom_call" | custom-call | tf_op jit(solution)/shard_map/pallas_call | solution.py:496

commit v5 on v4

--- a/solution.py
+++ b/solution.py
@@ -12,6 +12,7 @@
 MESH = pl.DeviceIdType.MESH
 
 NY, NX, NZ = 4, 4, 4
+FAR_FIRST = (2, 1, 3)
 CHUNK = 64
 STAGES = ("P1", "P2", "P3", "P4", "P5", "P6A", "P6", "P7", "P8", "P8A", "P9", "P10", "P11", "P12")
 SCHEDULE = (
@@ -141,10 +142,8 @@
 
     def everyone(kind, k, buf, slots):
         slots[lay] = buf[piece(k, y)]
-        for dzl in range(2):
-            for o in range(NY):
-                if dzl or o:
-                    send(kind, k, buf.at[piece(k, (y + o) % NY)], slots.at[lay], dev(dzl=dzl, dy=o))
+        for dzl, o in ((1, 2), (0, 2), (1, 1), (1, 3), (0, 1), (0, 3), (1, 0)):
+            send(kind, k, buf.at[piece(k, (y + o) % NY)], slots.at[lay], dev(dzl=dzl, dy=o))
 
     def total(slots):
         v = slots[0].astype(F32)
@@ -156,7 +155,7 @@
         if k in PRE_DIRECT:
             everyone("D1", k, psb, rd1.at[k])
             return
-        for o in range(1, NY):
+        for o in FAR_FIRST:
             send("YR", k, ps.at[piece(k, (y + o) % NY)], ry.at[k, o - 1], dev(dy=o))
 
     def p2(k):
@@ -175,7 +174,7 @@
         t = jnp.tanh(A0 * (v * (1.0 + A1 * v2)))
         h = 0.5 * (1.0 + t)
         acts[piece(k, y), pl.ds(0, feats)] = (v * h).astype(BF)
-        for o in range(1, NY):
+        for o in FAR_FIRST:
             r = acts.at[piece(k, y), pl.ds(0, feats)]
             send("YA", k, r, r, dev(dy=o))
         gpr[k] = h + 0.5 * v * (1.0 - t * t) * (A0 * (1.0 + 3.0 * A1 * v2))
@@ -224,7 +223,7 @@
         zown[s] = first[:, :blk]
         zsend[s, pl.ds(0, hg)] = first.astype(BF)
         zsend[s, pl.ds(hg, hg)] = second.astype(BF)
-        for p in range(1, NZ):
+        for p in FAR_FIRST:
             send("ZR", k, zsend.at[s, pl.ds(p * blk, blk)], rz.at[k, p - 1], dev(dzh=p))
 
     def p7(k):
@@ -238,7 +237,7 @@
 
         err = recon + decb_v[...] - tgt[s].astype(F32)
         eall[s, pl.ds(0, blk)] = err.astype(BF)
-        for p in range(1, NZ):
+        for p in FAR_FIRST:
             send("ZA", k, eall.at[s, pl.ds(0, blk)], eall.at[s, pl.ds((NZ - p) * blk, blk)], dev(dzh=p))
         bsum[...] += fold(err)
         sq[...] += fold(err * err)
@@ -291,7 +290,7 @@
         if k in BACK_DIRECT:
             everyone("D2", k, by, rd2.at[k])
             return
-        for o in range(1, NY):
+        for o in FAR_FIRST:
             send("YB", k, by.at[piece(k, (y + o) % NY)], ryb.at[k, o - 1], dev(dy=o))
 
     def p11(k):
@@ -311,7 +310,7 @@
             dpre = (zs_b[k] + zr_b[k]) * gpr[k]
         r = dall.at[piece(k, y)]
         dall[piece(k, y)] = dpre.astype(BF)
-        for o in range(1, NY):
+        for o in FAR_FIRST:
             send("YD", k, r, r, dev(dy=o))
         pb[...] += fold(dpre)
 

time: 86.3 us -> 85 us (0.985)
  Pallas kernels: 83.7 us -> 82.5 us
    pallas_call x1, Pallas kernels: 81.3 us -> 80.1 us  [shards(): pl.pallas_call(kernel, out_shape=(jax.ShapeDtypeStruct((depth, feats), F3...]
where the time goes in v5:
time: 85 us; the launch traced here: 84.9 us
  Pallas kernels  82.5 us (97%)
  between operations  2.41 us (3%)
    pallas_call x1, Pallas kernels, shards(): pl.pallas_call(kernel, out_shape=(jax.ShapeDtypeStruct((depth, feats), F3...  80.1 us
    pallas_call x1, Pallas kernels, shards(): pl.pallas_call(place, out_shape=tuple((pltpu.HBM(v.shape, v.dtype) for v...  2.41 us

profile of v5, /device:TPU:1, one launch (start us, length us, event | category | flops | bytes accessed | tf_op | source)
XLA Modules:
  0.0 84.9 jit_solution(3383383408993487380)
XLA Ops:
  0.6 80.1 %shard_map.101 = (f32[512,512]{1,0:T(8,128)S(1)}, f32[1,512]{1,0:T(1,128)S(1)}, bf16[1,512,4096]{2,1,0:T(8,128)(2,1)S(1)}, f32[1,128]{1,0:T(1,128)S(1)}, f32[1,1]{1,0:T(1,128)}) custom-call(bf16[512,512]{1,0:T(8,128)(2,1)} %src_h.1, bf16[512,512]{1,0:T(8,128)(2,1)} %enc_h.1, f32[1,512]{1,0:T(1,128)} %bitcast.3, bf16[1,512,4096]{2,1,0:T(8,128)(2,1)} %w_h.1, ...), custom_call_target="tpu_custom_call" | custom-call | tf_op jit(solution)/shard_map/pallas_call | solution.py:480
  80.7 2.4 %shard_map.102 = (f32[512,512]{1,0:T(8,128)}, f32[1,512]{1,0:T(1,128)}, bf16[1,512,4096]{2,1,0:T(8,128)(2,1)}, f32[1,128]{1,0:T(1,128)}) custom-call(f32[512,512]{1,0:T(8,128)S(1)} %get-tuple-element.14.a, f32[1,512]{1,0:T(1,128)S(1)} %get-tuple-element.15.b, bf16[1,512,4096]{2,1,0:T(8,128)(2,1)S(1)} %get-tuple-element.16.c, f32[1,128]{1,0:T(1,128)S(1)} %get-tuple-element.17.d), custom_call_target="tpu_custom_call" | custom-call | tf_op jit(solution)/shard_map/pallas_call | solution.py:495
